TPU v7x, 32 devices: a whole 2x2x4 slice. The times are simulated.
32 devices in a mesh: aux: 4 (over y, x), vir: 8 (over z, core).
Axes of the slice: x: 2, y: 2, z: 4, core: 2. Of those that a mesh axis runs over, the one named last changes fastest.
Arguments:
- orbitals: bfloat16 [8192, 2, 4096], P('aux', None, 'vir'), may hold values from -0.5390625 to 0.5390625
- screened: bfloat16 [8192, 8192], P('vir', 'aux'), may hold values from -0.0625 to 0.0625
- density_in: float32 [4096, 4096], P('aux', 'vir'), may hold values from -6 to 6
Outputs:
- density: float32 [4096, 4096], P('aux', 'vir')
All inputs are finite; a program needn't handle non-finite values.
Results may differ from a plain program's by a relative error of at most 0.008.
Values may be sent and summed in bfloat16 or wider, within the bound.
A program may use at most 192 MiB of HBM per device.

v0:
```python
import jax
import jax.numpy as jnp
from jax import lax
from jax.sharding import PartitionSpec as P


def shards(orbitals, screened, density_in):
    row_count, occ_count, col_count = orbitals.shape
    gathered = lax.all_gather(orbitals, "aux", axis=0, tiled=True)
    all_rows = gathered.reshape(gathered.shape[0], occ_count * col_count)
    screened_sum = lax.dot_general(
        lax.all_gather(screened, "vir", axis=0, tiled=True),
        all_rows,
        (((0,), (0,)), ((), ())),
        preferred_element_type=jnp.float32,
    )
    screened_orb = screened_sum.astype(jnp.bfloat16).reshape(row_count * occ_count, col_count)
    all_cols = lax.all_gather(orbitals, "vir", axis=2, tiled=True)
    all_cols = all_cols.reshape(row_count * occ_count, all_cols.shape[2])
    partial_value = lax.dot_general(
        all_cols, screened_orb, (((0,), (0,)), ((), ())), preferred_element_type=jnp.float32
    )
    summed = lax.psum_scatter(
        partial_value.astype(jnp.bfloat16), "aux", scatter_dimension=0, tiled=True
    ).astype(jnp.float32)
    return density_in + summed


def solution(mesh):
    return jax.shard_map(
        shards,
        mesh=mesh,
        in_specs=(P("aux", None, "vir"), P("vir", "aux"), P("aux", "vir")),
        out_specs=P("aux", "vir"),
        check_vma=False,
    )
```

profile of v0, /device:TPU:0, one launch (start us, length us, event | category | flops | bytes accessed | tf_op | source)
XLA Modules:
  0.0 886.5 jit_solution(6331638470191776095)
XLA Ops:
  6.5 0.0 all-gather.6.cloned.1.call-start
  6.5 0.7 all-gather.6.cloned.1.call-update
  7.3 0.0 all-gather.4.cloned.1.call-start
  7.3 0.7 all-gather.4.cloned.1.call-update
  8.0 0.0 all-gather.8.cloned.1.call-start
  8.1 0.7 all-gather.8.cloned.1.call-update
  8.7 0.0 reduce-scatter.2.cloned.1.call-start
  8.8 160.6 %all-gather.6.cloned.1.call-done = bf16[8192,2,512]{2,1,0:T(2,128)(2,1)} async-done(((bf16[2048,2,512]{2,1,0:T(2,128)(2,1)}), bf16[8192,2,512]{2,1,0:T(2,128)(2,1)}) %all-gather.6.cloned.1.call-update) | async-done | bytes 16777232 | tf_op jit(solution)/shard_map/all_gather | solution.py:9
  169.3 17.3 %copy.8 = bf16[1024,8,2,512]{3,1,2,0:T(8,128)(2,1)} copy(bf16[1024,8,2,512]{3,2,1,0:T(2,128)(2,1)} %bitcast.8) | data formatting | bytes 33554432
  186.6 273.0 %all-gather.4.cloned.1.call-done = bf16[8192,2048]{1,0:T(8,128)(2,1)} async-done(((bf16[1024,2048]{1,0:T(8,128)(2,1)}), bf16[8192,2048]{1,0:T(8,128)(2,1)}) %all-gather.4.cloned.1.call-update) | async-done | bytes 33554448 | tf_op jit(solution)/shard_map/all_gather | solution.py:12
  459.6 45.5 %convolution_convert_fusion.1 = bf16[2048,1024]{1,0:T(8,128)(2,1)} fusion(bf16[8192,2048]{1,0:T(8,128)(2,1)} %all-gather.4.cloned.1.call-done, bf16[8192,1024]{1,0:T(8,128)(2,1)} %bitcast.9), kind=kOutput, calls=%fused_computation.2 | convolution fusion | flops 34361835520 | bytes 54525952 | tf_op jit(solution)/shard_map/dot_general | solution.py:11
  505.1 7.1 reshape.10
  512.2 237.6 %all-gather.8.cloned.1.call-done = bf16[2048,2,4096]{2,1,0:T(2,128)(2,1)} async-done(((bf16[2048,2,512]{2,1,0:T(2,128)(2,1)}), bf16[2048,2,4096]{2,1,0:T(2,128)(2,1)}) %all-gather.8.cloned.1.call-update) | async-done | bytes 33554448 | tf_op jit(solution)/shard_map/all_gather | solution.py:18
  749.9 48.5 %reshape.11 = bf16[4096,4096]{1,0:T(8,128)(2,1)} reshape(bf16[2048,2,4096]{2,1,0:T(2,128)(2,1)} %all-gather.8.cloned.1.call-done) | data formatting | bytes 67108864 | tf_op jit(solution)/shard_map/reshape | solution.py:19
  798.4 23.7 %fusion = bf16[4096,512]{0,1:T(8,128)(2,1)} fusion(bf16[4096,512]{1,0:T(8,128)(2,1)} %reshape.10, bf16[4096,4096]{1,0:T(8,128)(2,1)} %reshape.11), kind=kOutput, calls=%fused_computation.1 | convolution fusion | flops 17181966336 | bytes 41943040 | tf_op jit(solution)/shard_map/dot_general | solution.py:20
  822.1 0.0 reduce-scatter.2.cloned.1.call-update
  822.1 1.9 copy.6
  824.1 50.1 %reduce-scatter.2.cloned.1.call-done = bf16[1024,512]{0,1:T(8,128)(2,1)} async-done(((bf16[4096,512]{0,1:T(8,128)(2,1)}), bf16[1024,512]{0,1:T(8,128)(2,1)}) %reduce-scatter.2.cloned.1.call-update) | async-done | bytes 1048592 | tf_op jit(solution)/shard_map/reduce_scatter | solution.py:23
  874.2 2.8 convert_add_fusion
  877.0 2.9 copy.7
Async XLA Ops:
  6.5 162.8 %all-gather.6.cloned.1.call-start = ((), (), s32[]{:S(2)}) async-start(), calls=%async_computation.2 | async-start | bytes 20971520 | tf_op jit(solution)/shard_map/all_gather | solution.py:9
  7.3 452.3 %all-gather.4.cloned.1.call-start = ((), (), s32[]{:S(2)}) async-start(), calls=%async_computation.1 | async-start | bytes 37748736 | tf_op jit(solution)/shard_map/all_gather | solution.py:12
  8.0 741.9 %all-gather.8.cloned.1.call-start = ((), (), s32[]{:S(2)}) async-start(), calls=%async_computation.3 | async-start | bytes 37748736 | tf_op jit(solution)/shard_map/all_gather | solution.py:18
  8.7 865.5 %reduce-scatter.2.cloned.1.call-start = ((), (), s32[]{:S(2)}) async-start(), calls=%async_computation.4 | async-start | bytes 5242880 | tf_op jit(solution)/shard_map/reduce_scatter | solution.py:23
Sparse Core Ops, SparseCore 0:
  9.2 160.1 all-gather.5
  170.9 288.6 all-gather.3
  461.2 288.6 all-gather.7
  822.3 51.8 reduce-scatter.1
where the time goes:
time: 888 us; the launch traced here: 886 us
  waiting for transfers between devices  723 us (81%)
  local copies, waits for them, and re-layouts  77.6 us (9%)
  matrix products  69.3 us (8%)
  between operations  13.1 us (1%)
    all_gather x1, waiting for transfers between devices, shards(): lax.all_gather(screened, 'vir', axis=0, tiled=True)  273 us
    all_gather x1, waiting for transfers between devices, shards(): all_cols = lax.all_gather(orbitals, 'vir', axis=2, tiled=True)  238 us
    all_gather x1, waiting for transfers between devices, shards(): gathered = lax.all_gather(orbitals, 'aux', axis=0, tiled=True)  161 us
    reduce_scatter x1, waiting for transfers between devices, shards(): lax.psum_scatter(partial_value.astype(jnp.bfloat16), 'aux', scatter_dimen...  50.1 us
    reshape x1, local copies, waits for them, and re-layouts, shards(): all_cols = all_cols.reshape(row_count * occ_count, all_cols.shape[2])  48.5 us
    dot_general x1, matrix products, shards(): lax.dot_general(lax.all_gather(screened, 'vir', axis=0, tiled=True), all_...  45.5 us
    dot_general x1, matrix products, shards(): lax.dot_general(all_cols, screened_orb, (((0,), (0,)), ((), ())), preferr...  23.7 us
    unnamed x2, local copies, waits for them, and re-layouts  19.2 us
  transfers between devices with their start and end apart: 4, of which 4 were waited for; matrix products, arithmetic and copies ran while one was open for 8% of the time, Pallas kernels for 0%

commit v1 on v0

v1 whole, which is shorter than its diff:
```python
import jax
import jax.numpy as jnp
from jax import lax
from jax.sharding import PartitionSpec as P

CORES = 2
HALVES = 2


def tie(value, other):
    if other is None:
        return value
    return lax.optimization_barrier((value, other))[0]


def dot(left, right):
    return lax.dot_general(left, right, (((0,), (0,)), ((), ())), preferred_element_type=jnp.float32).astype(jnp.bfloat16)


def make(n_aux, n_vir):
    line = n_vir // CORES
    shift = line // 4
    inner = 2 * shift
    outer_to_inner = [(g, g + shift) for g in range(shift)] + [(g, g - shift) for g in range(line - shift, line)]

    def on_cores(pairs):
        return [(a * CORES + c, b * CORES + c) for a, b in pairs for c in range(CORES)]

    hand = on_cores(outer_to_inner)
    back = [(b, a) for a, b in hand]
    swap = [(v, v ^ 1) for v in range(shift * CORES, (line - shift) * CORES)]

    def turn(r):
        return on_cores([(shift + j, shift + (j + r) % inner) for j in range(inner)])

    def shards(orbitals, screened, density_in):
        rows, occ, cols = orbitals.shape
        part = cols // HALVES
        v = lax.axis_index("vir")
        g, c = v // CORES, v % CORES
        is_inner = (g >= shift) & (g < line - shift)
        partner = jnp.where(g < line // 2, g - shift, g + shift)

        by_occ = jnp.transpose(orbitals, (1, 0, 2))
        halves = [by_occ[:, :, h * part : (h + 1) * part].reshape(occ * rows, part) for h in range(HALVES)]

        out_w = lax.ppermute(screened, "vir", hand)
        out_halves = []
        last = out_w
        for h in range(HALVES):
            last = lax.ppermute(tie(halves[h], last), "vir", hand)
            out_halves.append(last)

        flight = [None, None]

        def rotate(value, r):
            got = lax.ppermute(tie(value, flight[-2]), "vir", turn(r))
            flight.append(got)
            return got

        def source(r):
            own = shift + lax.rem(g - shift - r + 2 * inner, inner)
            return own, jnp.where(own < line // 2, own - shift, own + shift)

        w_pieces = [(g, screened), (partner, out_w)]
        for r in range(1, inner):
            own, far = source(r)
            w_pieces.append((own, rotate(screened, r)))
            w_pieces.append((far, rotate(out_w, r)))
        b_pieces = []
        for h in range(HALVES):
            b_pieces.append([(g, halves[h]), (partner, out_halves[h])])
            for r in range(1, inner):
                own, far = source(r)
                b_pieces[h].append((own, rotate(halves[h], r)))
                b_pieces[h].append((far, rotate(out_halves[h], r)))

        depth = screened.shape[0]
        w_all = jnp.zeros((depth * n_vir, screened.shape[1]), screened.dtype)
        for place, piece in w_pieces:
            other = lax.ppermute(piece, "vir", swap)
            w_all = lax.dynamic_update_slice(w_all, piece, ((place * CORES + c) * depth, 0))
            w_all = lax.dynamic_update_slice(w_all, other, ((place * CORES + 1 - c) * depth, 0))

        def screen(col_halves):
            return jnp.concatenate(
                [
                    dot(
                        w_all,
                        lax.all_gather(
                            jnp.concatenate([x[i * rows : (i + 1) * rows] for x in col_halves], axis=1),
                            "aux",
                            axis=0,
                            tiled=True,
                        ),
                    )
                    for i in range(occ)
                ],
                axis=0,
            )

        right = [screen(halves), screen(out_halves)]

        summed = [[], []]
        for h in range(HALVES):
            left = [(place * CORES + c, piece) for place, piece in b_pieces[h]]
            left += [(place * CORES + 1 - c, lax.ppermute(piece, "vir", swap)) for place, piece in b_pieces[h]]
            for side in (1, 0):
                tiles = jnp.zeros((n_vir, part, cols), jnp.bfloat16)
                for place, piece in left:
                    tiles = lax.dynamic_update_slice(tiles, dot(piece, right[side])[None], (place, 0, 0))
                mine = lax.psum_scatter(tiles, "aux", scatter_dimension=0, tiled=True)
                if side == 1:
                    mine = lax.ppermute(mine, "vir", back)
                summed[side].append(mine)
        total = [jnp.stack(x, axis=1).reshape(density_in.shape) for x in summed]
        return density_in + jnp.where(is_inner, total[0], total[1]).astype(jnp.float32)

    return shards


def solution(mesh):
    return jax.shard_map(
        make(mesh.shape["aux"], mesh.shape["vir"]),
        mesh=mesh,
        in_specs=(P("aux", None, "vir"), P("vir", "aux"), P("aux", "vir")),
        out_specs=P("aux", "vir"),
        check_vma=False,
    )
```

time: 888 us -> 790 us (0.89)
  waiting for transfers between devices: 723 us -> 423 us
  matrix products: 69.3 us -> 199 us
  starting transfers between devices: 0.12 us -> 60.6 us
    all_gather x3 -> x4, waiting for transfers between devices: 671 us -> 129 us  [screen(): lax.all_gather(jnp.concatenate([x[i * rows:(i + 1) * rows] for x in col_h...]
    ppermute x0 -> x23, waiting for transfers between devices: none -> 167 us  [the longest x1 84.4 us: shards(): out_w = lax.ppermute(screened, 'vir', hand)]
    dot_general x2 -> x36, matrix products: 69.3 us -> 199 us  [dot(): lax.dot_general(left, right, (((0,), (0,)), ((), ())), preferred_element_...]
    reduce_scatter x1 -> x4, waiting for transfers between devices: 50.1 us -> 127 us  [shards(): mine = lax.psum_scatter(tiles, 'aux', scatter_dimension=0, tiled=True)]
    ppermute x0 -> x23, starting transfers between devices: none -> 59.9 us  [the longest x8 16.1 us: shards(): lax.ppermute(piece, 'vir', swap)]
    reshape x2 -> x0, local copies, waits for them, and re-layouts: 55.6 us -> none  [the longest x1 48.5 us: shards(): all_cols = all_cols.reshape(row_count * occ_count, all_cols.shape[2])]
    dynamic_update_slice x0 -> x16, local copies, waits for them, and re-layouts: none -> 34.4 us  [the longest x4 19.1 us: shards(): lax.dynamic_update_slice(w_all, other, ((place * CORES + 1 - c) * depth, 0))]
    broadcast_in_dim x0 -> x9, local copies, waits for them, and re-layouts: none -> 12.8 us  [the longest x1 11.7 us: shards(): w_all = jnp.zeros((depth * n_vir, screened.shape[1]), screened.dtype)]
  transfers between devices with their start and end apart: 4 -> 31, of which waited for: 4 -> 10; matrix products, arithmetic and copies ran while one was open for 8% -> 33% of each run, Pallas kernels for 0% -> 0%
where the time goes in v1:
time: 790 us; the launch traced here: 783 us
  waiting for transfers between devices  423 us (54%)
  matrix products  199 us (25%)
  local copies, waits for them, and re-layouts  75.9 us (10%)
  starting transfers between devices  60.6 us (8%)
  between operations  14.7 us (2%)
  other arithmetic  9.16 us (1%)
    dot_general x36, matrix products, dot(): lax.dot_general(left, right, (((0,), (0,)), ((), ())), preferred_element_...  199 us
    all_gather x4, waiting for transfers between devices, screen(): lax.all_gather(jnp.concatenate([x[i * rows:(i + 1) * rows] for x in col_h...  129 us
    reduce_scatter x4, waiting for transfers between devices, shards(): mine = lax.psum_scatter(tiles, 'aux', scatter_dimension=0, tiled=True)  127 us
    ppermute x1, waiting for transfers between devices, shards(): out_w = lax.ppermute(screened, 'vir', hand)  84.4 us
    ppermute x2, waiting for transfers between devices, shards(): last = lax.ppermute(tie(halves[h], last), 'vir', hand)  83.1 us
    unnamed x61, local copies, waits for them, and re-layouts  20.3 us
    dynamic_update_slice x4, local copies, waits for them, and re-layouts, shards(): lax.dynamic_update_slice(w_all, other, ((place * CORES + 1 - c) * depth, 0))  19.1 us
    ppermute x8, starting transfers between devices, shards(): lax.ppermute(piece, 'vir', swap)  16.1 us
  transfers between devices with their start and end apart: 31, of which 10 were waited for; matrix products, arithmetic and copies ran while one was open for 33% of the time, Pallas kernels for 0%

profile of v1, /device:TPU:0, one launch (start us, length us, event | category | flops | bytes accessed | tf_op | source)
XLA Modules:
  0.0 782.6 jit_solution(9419117204900470163)
XLA Ops:
  6.5 5.2 collective-permute-start.1
  11.7 2.9 copy.52
  17.2 84.4 %collective-permute-done.1 = bf16[1024,2048]{1,0:T(8,128)(2,1)S(1)} collective-permute-done((bf16[1024,2048]{1,0:T(8,128)(2,1)}, bf16[1024,2048]{1,0:T(8,128)(2,1)S(1)}, u32[]{:S(2)}, u32[]{:S(2)}) %collective-permute-start.1) | collective-permute-done | bytes 4194336 | tf_op jit(solution)/shard_map/ppermute | solution.py:47
  101.6 5.6 collective-permute-start.7
  107.2 42.7 %collective-permute-done.7 = bf16[4096,256]{1,0:T(8,128)(2,1)} collective-permute-done((bf16[4096,256]{1,0:T(8,128)(2,1)S(1)}, bf16[4096,256]{1,0:T(8,128)(2,1)}, u32[]{:S(2)}, u32[]{:S(2)}) %collective-permute-start.7) | collective-permute-done | bytes 2097184 | tf_op jit(solution)/shard_map/ppermute | solution.py:51
  149.9 5.8 collective-permute-start.14
  157.4 40.4 %collective-permute-done.14 = bf16[4096,256]{1,0:T(8,128)(2,1)} collective-permute-done((bf16[4096,256]{1,0:T(8,128)(2,1)}, bf16[4096,256]{1,0:T(8,128)(2,1)}, u32[]{:S(2)}, u32[]{:S(2)}) %collective-permute-start.14) | collective-permute-done | bytes 2097184 | tf_op jit(solution)/shard_map/ppermute | solution.py:51
  206.6 2.7 collective-permute-start.3
  209.2 2.7 collective-permute-start.5
  211.9 2.8 collective-permute-start
  214.7 2.7 collective-permute-start.2
  217.4 2.7 collective-permute-start.4
  220.0 2.7 collective-permute-start.6
  229.7 11.7 %broadcast_in_dim.99 = bf16[8192,2048]{1,0:T(8,128)(2,1)} broadcast(bf16[]{:T(256)} %constant.46.clone.1), dimensions={} | broadcast | bytes 33554432 | tf_op jit(solution)/shard_map/broadcast_in_dim | solution.py:79
  241.4 3.1 constant_dynamic-update-slice_fusion.15
  244.5 4.9 constant_dynamic-update-slice_fusion.14
  255.8 4.7 constant_dynamic-update-slice_fusion.12
  260.5 4.8 constant_dynamic-update-slice_fusion.11
  267.3 4.7 constant_dynamic-update-slice_fusion.10
  272.0 4.8 constant_dynamic-update-slice_fusion.9
  278.8 2.6 collective-permute-start.16
  281.4 4.8 constant_dynamic-update-slice_fusion.8
  286.2 3.7 all-gather.11.cloned.1.call-done
  289.9 24.7 %convolution_convert_fusion = bf16[2048,512]{1,0:T(8,128)(2,1)} fusion(bf16[8192,2048]{1,0:T(8,128)(2,1)} %constant_dynamic-update-slice_fusion.8, bf16[8192,512]{1,0:T(8,128)(2,1)} %all-gather.11.cloned.1.call-done), kind=kOutput, calls=%fused_computation.3 | convolution fusion | flops 17180917760 | bytes 44040192 | tf_op jit(solution)/shard_map/dot_general | solution.py:17
  314.5 64.8 %all-gather.9.cloned.1.call-done = bf16[8192,512]{1,0:T(8,128)(2,1)} async-done(((bf16[2048,512]{1,0:T(8,128)(2,1)}), bf16[8192,512]{1,0:T(8,128)(2,1)}) %all-gather.9.cloned.1.call-update) | async-done | bytes 8388624 | tf_op jit(solution)/shard_map/all_gather | solution.py:90
  379.4 24.0 %convolution_convert_fusion.1 = bf16[2048,512]{1,0:T(8,128)(2,1)S(1)} fusion(bf16[8192,2048]{1,0:T(8,128)(2,1)} %constant_dynamic-update-slice_fusion.8, bf16[8192,512]{1,0:T(8,128)(2,1)} %all-gather.9.cloned.1.call-done), kind=kOutput, calls=%fused_computation.4 | convolution fusion | flops 17180917760 | bytes 44040192 | tf_op jit(solution)/shard_map/dot_general | solution.py:17
  408.2 4.3 fusion.35
  414.1 2.8 fusion.30
  417.1 4.3 fusion.32
  421.4 3.5 fusion.34
  427.1 2.9 fusion.37
  436.0 2.8 fusion.39
  438.8 2.9 fusion.41
  443.2 25.6 %all-gather.5.cloned.1.call-done = bf16[8192,512]{1,0:T(8,128)(2,1)} async-done(((bf16[2048,512]{1,0:T(8,128)(2,1)}), bf16[8192,512]{1,0:T(8,128)(2,1)}) %all-gather.5.cloned.1.call-update) | async-done | bytes 8388624 | tf_op jit(solution)/shard_map/all_gather | solution.py:90
  468.9 24.8 %convolution_convert_fusion.3 = bf16[2048,512]{1,0:T(8,128)(2,1)} fusion(bf16[8192,2048]{1,0:T(8,128)(2,1)} %constant_dynamic-update-slice_fusion.8, bf16[8192,512]{1,0:T(8,128)(2,1)} %all-gather.5.cloned.1.call-done), kind=kOutput, calls=%fused_computation.6 | convolution fusion | flops 17180917760 | bytes 44040192 | tf_op jit(solution)/shard_map/dot_general | solution.py:17
  493.7 2.9 fusion.42
  496.7 4.3 fusion.49
  502.6 2.9 fusion.44
  505.7 4.3 fusion.46
  510.0 3.3 fusion.48
  513.4 2.9 fusion.51
  516.2 2.9 fusion.53
  519.1 2.9 fusion.55
  523.6 34.7 %all-gather.7.cloned.1.call-done = bf16[8192,512]{1,0:T(8,128)(2,1)} async-done(((bf16[2048,512]{1,0:T(8,128)(2,1)}), bf16[8192,512]{1,0:T(8,128)(2,1)}) %all-gather.7.cloned.1.call-update) | async-done | bytes 8388624 | tf_op jit(solution)/shard_map/all_gather | solution.py:90
  558.2 24.0 %convolution_convert_fusion.2 = bf16[2048,512]{1,0:T(8,128)(2,1)S(1)} fusion(bf16[8192,2048]{1,0:T(8,128)(2,1)} %constant_dynamic-update-slice_fusion.8, bf16[8192,512]{1,0:T(8,128)(2,1)} %all-gather.7.cloned.1.call-done), kind=kOutput, calls=%fused_computation.5 | convolution fusion | flops 17180917760 | bytes 44040192 | tf_op jit(solution)/shard_map/dot_general | solution.py:17
  583.6 3.0 fusion.7
  586.8 3.5 fusion
  592.0 3.6 fusion.2
  595.7 2.9 fusion.4
  598.5 2.9 fusion.6
  601.4 2.9 fusion.9
  604.3 2.9 fusion.11
  607.2 2.9 fusion.13
  611.7 4.2 fusion.21
  616.0 4.2 fusion.14
  622.0 3.7 fusion.16
  625.7 2.9 fusion.18
  628.6 2.9 fusion.20
  631.4 2.9 fusion.23
  634.3 2.9 fusion.25
  637.2 2.9 fusion.27
  642.7 35.6 %reduce-scatter.11.cloned.1.call-done = bf16[2,256,512]{2,1,0:T(8,128)(2,1)} async-done(((bf16[8,256,512]{2,1,0:T(8,128)(2,1)}), bf16[2,256,512]{2,1,0:T(8,128)(2,1)}) %reduce-scatter.11.cloned.1.call-update) | async-done | bytes 524304 | tf_op jit(solution)/shard_map/reduce_scatter | solution.py:112
  679.6 52.4 %reduce-scatter.5.cloned.1.call-done = bf16[2,256,512]{2,1,0:T(8,128)(2,1)} async-done(((bf16[8,256,512]{2,1,0:T(8,128)(2,1)}), bf16[2,256,512]{2,1,0:T(8,128)(2,1)}) %reduce-scatter.5.cloned.1.call-update) | async-done | bytes 524304 | tf_op jit(solution)/shard_map/reduce_scatter | solution.py:112
  732.1 38.4 %reduce-scatter.7.cloned.1.call-done = bf16[2,256,512]{2,1,0:T(8,128)(2,1)} async-done(((bf16[8,256,512]{2,1,0:T(8,128)(2,1)}), bf16[2,256,512]{2,1,0:T(8,128)(2,1)}) %reduce-scatter.7.cloned.1.call-update) | async-done | bytes 524304 | tf_op jit(solution)/shard_map/reduce_scatter | solution.py:112
  (143 shorter events, 65.6 us)
Async XLA Ops:
  6.5 283.3 %all-gather.11.cloned.1.call-start = ((), (), s32[]{:S(2)}) async-start(), calls=%async_computation.9 | async-start | bytes 10485760 | tf_op jit(solution)/shard_map/all_gather | solution.py:90
  6.5 95.1 %collective-permute-start.1 = (bf16[1024,2048]{1,0:T(8,128)(2,1)}, bf16[1024,2048]{1,0:T(8,128)(2,1)S(1)}, u32[]{:S(2)}, u32[]{:S(2)}) collective-permute-start(bf16[1024,2048]{1,0:T(8,128)(2,1)} %param.4), channel_id=1, source_target_pairs={{0,2},{1,3},{6,4},{7,5},{8,10},{9,11},{14,12},{15,13},{16,18},{17,... | collective-permute-start | bytes 12582920 | tf_op jit(solution)/shard_map/ppermute | solution.py:47
  14.6 2.6 copy-start
  17.2 180.5 %copy-start.9 = (bf16[2,2048,256]{2,1,0:T(8,128)(2,1)}, bf16[2,2048,256]{2,1,0:T(8,128)(2,1)S(1)}, u32[]{:S(2)}) copy-start(bf16[2,2048,256]{2,1,0:T(8,128)(2,1)S(1)} %get-tuple-element.17) | copy-start | bytes 6291460
  101.6 55.8 %copy-start.6 = (bf16[1024,2048]{1,0:T(8,128)(2,1)}, bf16[1024,2048]{1,0:T(8,128)(2,1)S(1)}, u32[]{:S(2)}) copy-start(bf16[1024,2048]{1,0:T(8,128)(2,1)S(1)} %collective-permute-done.1) | copy-start | bytes 12582916
  101.6 48.3 %collective-permute-start.7 = (bf16[4096,256]{1,0:T(8,128)(2,1)S(1)}, bf16[4096,256]{1,0:T(8,128)(2,1)}, u32[]{:S(2)}, u32[]{:S(2)}) collective-permute-start(bf16[4096,256]{1,0:T(8,128)(2,1)S(1)} %bitcast.189), channel_id=1, source_target_pairs={{0,2},{1,3},{6,4},{7,5},{8,10},{9,11},{14,12},{15,13},{16,18},{17,... | collective-permute-start | bytes 6291464 | tf_op jit(solution)/shard_map/ppermute | solution.py:51
  149.9 47.9 %collective-permute-start.14 = (bf16[4096,256]{1,0:T(8,128)(2,1)}, bf16[4096,256]{1,0:T(8,128)(2,1)}, u32[]{:S(2)}, u32[]{:S(2)}) collective-permute-start(bf16[4096,256]{1,0:T(8,128)(2,1)} %bitcast.17), channel_id=1, source_target_pairs={{0,2},{1,3},{6,4},{7,5},{8,10},{9,11},{14,12},{15,13},{16,18},{17,... | collective-permute-start | bytes 6291464 | tf_op jit(solution)/shard_map/ppermute | solution.py:51
  201.0 178.4 %all-gather.9.cloned.1.call-start = ((), (), s32[]{:S(2)}) async-start(), calls=%async_computation.8 | async-start | bytes 10485760 | tf_op jit(solution)/shard_map/all_gather | solution.py:90
  202.5 266.3 %all-gather.5.cloned.1.call-start = ((), (), s32[]{:S(2)}) async-start(), calls=%async_computation.4 | async-start | bytes 10485760 | tf_op jit(solution)/shard_map/all_gather | solution.py:90
  206.5 351.7 %all-gather.7.cloned.1.call-start = ((), (), s32[]{:S(2)}) async-start(), calls=%async_computation.5 | async-start | bytes 10485760 | tf_op jit(solution)/shard_map/all_gather | solution.py:90
  206.6 10.8 %collective-permute-start.3 = (bf16[1024,2048]{1,0:T(8,128)(2,1)}, bf16[1024,2048]{1,0:T(8,128)(2,1)}, u32[]{:S(2)}, u32[]{:S(2)}) collective-permute-start(bf16[1024,2048]{1,0:T(8,128)(2,1)} %param.4), channel_id=1, source_target_pairs={{2,4},{3,5},{4,2},{5,3},{10,12},{11,13},{12,10},{13,11},{18,20},{1... | collective-permute-start | bytes 12582920 | tf_op jit(solution)/shard_map/ppermute | solution.py:57
  209.2 10.8 %collective-permute-start.5 = (bf16[1024,2048]{1,0:T(8,128)(2,1)}, bf16[1024,2048]{1,0:T(8,128)(2,1)}, u32[]{:S(2)}, u32[]{:S(2)}) collective-permute-start(bf16[1024,2048]{1,0:T(8,128)(2,1)} %copy-done.6), channel_id=1, source_target_pairs={{2,4},{3,5},{4,2},{5,3},{10,12},{11,13},{12,10},{13,11},{18,20},{1... | collective-permute-start | bytes 12582920 | tf_op jit(solution)/shard_map/ppermute | solution.py:57
  211.9 15.8 %collective-permute-start = (bf16[1024,2048]{1,0:T(8,128)(2,1)}, bf16[1024,2048]{1,0:T(8,128)(2,1)}, u32[]{:S(2)}, u32[]{:S(2)}) collective-permute-start(bf16[1024,2048]{1,0:T(8,128)(2,1)} %param.4), channel_id=1, source_target_pairs={{2,3},{3,2},{4,5},{5,4},{10,11},{11,10},{12,13},{13,12},{18,19},{1... | collective-permute-start | bytes 12582920 | tf_op jit(solution)/shard_map/ppermute | solution.py:81
  214.7 39.1 %collective-permute-start.2 = (bf16[1024,2048]{1,0:T(8,128)(2,1)}, bf16[1024,2048]{1,0:T(8,128)(2,1)}, u32[]{:S(2)}, u32[]{:S(2)}) collective-permute-start(bf16[1024,2048]{1,0:T(8,128)(2,1)} %copy-done.6), channel_id=1, source_target_pairs={{2,3},{3,2},{4,5},{5,4},{10,11},{11,10},{12,13},{13,12},{18,19},{1... | collective-permute-start | bytes 12582920 | tf_op jit(solution)/shard_map/ppermute | solution.py:81
  217.4 47.9 %collective-permute-start.4 = (bf16[1024,2048]{1,0:T(8,128)(2,1)}, bf16[1024,2048]{1,0:T(8,128)(2,1)}, u32[]{:S(2)}, u32[]{:S(2)}) collective-permute-start(bf16[1024,2048]{1,0:T(8,128)(2,1)} %collective-permute-done.3), channel_id=1, source_target_pairs={{2,3},{3,2},{4,5},{5,4},{10,11},{11,10},{12,13},{13,12},{18,19},{1... | collective-permute-start | bytes 12582920 | tf_op jit(solution)/shard_map/ppermute | solution.py:81
  220.0 58.8 %collective-permute-start.6 = (bf16[1024,2048]{1,0:T(8,128)(2,1)}, bf16[1024,2048]{1,0:T(8,128)(2,1)}, u32[]{:S(2)}, u32[]{:S(2)}) collective-permute-start(bf16[1024,2048]{1,0:T(8,128)(2,1)} %collective-permute-done.5), channel_id=1, source_target_pairs={{2,3},{3,2},{4,5},{5,4},{10,11},{11,10},{12,13},{13,12},{18,19},{1... | collective-permute-start | bytes 12582920 | tf_op jit(solution)/shard_map/ppermute | solution.py:81
  224.2 1.6 copy-start.10
  224.2 417.2 %reduce-scatter.9.cloned.1.call-start = ((), (), s32[]{:S(2)}) async-start(), calls=%async_computation.10 | async-start | bytes 2621440 | tf_op jit(solution)/shard_map/reduce_scatter | solution.py:112
  225.8 26.0 %collective-permute-start.8 = (bf16[4096,256]{1,0:T(8,128)(2,1)S(1)}, bf16[4096,256]{1,0:T(8,128)(2,1)}, u32[]{:S(2)}, u32[]{:S(2)}) collective-permute-start(bf16[4096,256]{1,0:T(8,128)(2,1)S(1)} %bitcast.190), channel_id=1, source_target_pairs={{2,4},{3,5},{4,2},{5,3},{10,12},{11,13},{12,10},{13,11},{18,20},{1... | collective-permute-start | bytes 6291464 | tf_op jit(solution)/shard_map/ppermute | solution.py:57
  227.8 49.0 %collective-permute-start.9 = (bf16[4096,256]{1,0:T(8,128)(2,1)}, bf16[4096,256]{1,0:T(8,128)(2,1)}, u32[]{:S(2)}, u32[]{:S(2)}) collective-permute-start(bf16[4096,256]{1,0:T(8,128)(2,1)} %collective-permute-done.7), channel_id=1, source_target_pairs={{2,4},{3,5},{4,2},{5,3},{10,12},{11,13},{12,10},{13,11},{18,20},{1... | collective-permute-start | bytes 6291464 | tf_op jit(solution)/shard_map/ppermute | solution.py:57
  229.7 11.7 %copy-start.5 = (bf16[1024,2048]{1,0:T(8,128)(2,1)S(1)}, bf16[1024,2048]{1,0:T(8,128)(2,1)}, u32[]{:S(2)}) copy-start(bf16[1024,2048]{1,0:T(8,128)(2,1)} %param.4) | copy-start | bytes 12582916
  244.5 4.9 copy-start.7
  251.8 154.4 %collective-permute-start.10 = (bf16[4096,256]{1,0:T(8,128)(2,1)S(1)}, bf16[4096,256]{1,0:T(8,128)(2,1)}, u32[]{:S(2)}, u32[]{:S(2)}) collective-permute-start(bf16[4096,256]{1,0:T(8,128)(2,1)S(1)} %bitcast.191), channel_id=1, source_target_pairs={{2,3},{3,2},{4,5},{5,4},{10,11},{11,10},{12,13},{13,12},{18,19},{1... | collective-permute-start | bytes 6291464 | tf_op jit(solution)/shard_map/ppermute | solution.py:107
  253.8 178.2 %collective-permute-start.15 = (bf16[4096,256]{1,0:T(8,128)(2,1)}, bf16[4096,256]{1,0:T(8,128)(2,1)}, u32[]{:S(2)}, u32[]{:S(2)}) collective-permute-start(bf16[4096,256]{1,0:T(8,128)(2,1)} %bitcast.17), channel_id=1, source_target_pairs={{2,4},{3,5},{4,2},{5,3},{10,12},{11,13},{12,10},{13,11},{18,20},{1... | collective-permute-start | bytes 6291464 | tf_op jit(solution)/shard_map/ppermute | solution.py:57
  265.3 159.6 %collective-permute-start.11 = (bf16[4096,256]{1,0:T(8,128)(2,1)}, bf16[4096,256]{1,0:T(8,128)(2,1)}, u32[]{:S(2)}, u32[]{:S(2)}) collective-permute-start(bf16[4096,256]{1,0:T(8,128)(2,1)} %collective-permute-done.7), channel_id=1, source_target_pairs={{2,3},{3,2},{4,5},{5,4},{10,11},{11,10},{12,13},{13,12},{18,19},{1... | collective-permute-start | bytes 6291464 | tf_op jit(solution)/shard_map/ppermute | solution.py:107
  276.8 153.2 %collective-permute-start.12 = (bf16[4096,256]{1,0:T(8,128)(2,1)}, bf16[4096,256]{1,0:T(8,128)(2,1)}, u32[]{:S(2)}, u32[]{:S(2)}) collective-permute-start(bf16[4096,256]{1,0:T(8,128)(2,1)} %collective-permute-done.8), channel_id=1, source_target_pairs={{2,3},{3,2},{4,5},{5,4},{10,11},{11,10},{12,13},{13,12},{18,19},{1... | collective-permute-start | bytes 6291464 | tf_op jit(solution)/shard_map/ppermute | solution.py:107
  278.8 155.1 %collective-permute-start.16 = (bf16[4096,256]{1,0:T(8,128)(2,1)}, bf16[4096,256]{1,0:T(8,128)(2,1)}, u32[]{:S(2)}, u32[]{:S(2)}) collective-permute-start(bf16[4096,256]{1,0:T(8,128)(2,1)} %collective-permute-done.14), channel_id=1, source_target_pairs={{2,4},{3,5},{4,2},{5,3},{10,12},{11,13},{12,10},{13,11},{18,20},{1... | collective-permute-start | bytes 6291464 | tf_op jit(solution)/shard_map/ppermute | solution.py:57
  379.4 25.4 %copy-start.15 = (bf16[2048,512]{1,0:T(8,128)(2,1)S(1)}, bf16[2048,512]{1,0:T(8,128)(2,1)}, u32[]{:S(2)}) copy-start(bf16[2048,512]{1,0:T(8,128)(2,1)} %convolution_convert_fusion) | copy-start | bytes 6291460
  403.4 1.4 copy-start.21
  406.2 32.6 %collective-permute-start.13 = (bf16[4096,256]{1,0:T(8,128)(2,1)}, bf16[4096,256]{1,0:T(8,128)(2,1)}, u32[]{:S(2)}, u32[]{:S(2)}) collective-permute-start(bf16[4096,256]{1,0:T(8,128)(2,1)} %collective-permute-done.9), channel_id=1, source_target_pairs={{2,3},{3,2},{4,5},{5,4},{10,11},{11,10},{12,13},{13,12},{18,19},{1... | collective-permute-start | bytes 6291464 | tf_op jit(solution)/shard_map/ppermute | solution.py:107
  408.2 4.5 copy-start.22
  412.5 1.6 copy-start.16
  417.1 4.3 copy-start.17
  417.1 4.3 copy-start.23
  424.9 71.8 %collective-permute-start.17 = (bf16[4096,256]{1,0:T(8,128)(2,1)}, bf16[4096,256]{1,0:T(8,128)(2,1)}, u32[]{:S(2)}, u32[]{:S(2)}) collective-permute-start(bf16[4096,256]{1,0:T(8,128)(2,1)} %bitcast.17), channel_id=1, source_target_pairs={{2,3},{3,2},{4,5},{5,4},{10,11},{11,10},{12,13},{13,12},{18,19},{1... | collective-permute-start | bytes 6291464 | tf_op jit(solution)/shard_map/ppermute | solution.py:107
  430.0 83.4 %collective-permute-start.18 = (bf16[4096,256]{1,0:T(8,128)(2,1)}, bf16[4096,256]{1,0:T(8,128)(2,1)}, u32[]{:S(2)}, u32[]{:S(2)}) collective-permute-start(bf16[4096,256]{1,0:T(8,128)(2,1)} %collective-permute-done.14), channel_id=1, source_target_pairs={{2,3},{3,2},{4,5},{5,4},{10,11},{11,10},{12,13},{13,12},{18,19},{1... | collective-permute-start | bytes 6291464 | tf_op jit(solution)/shard_map/ppermute | solution.py:107
  431.9 84.3 %collective-permute-start.19 = (bf16[4096,256]{1,0:T(8,128)(2,1)}, bf16[4096,256]{1,0:T(8,128)(2,1)}, u32[]{:S(2)}, u32[]{:S(2)}) collective-permute-start(bf16[4096,256]{1,0:T(8,128)(2,1)} %collective-permute-done.15), channel_id=1, source_target_pairs={{2,3},{3,2},{4,5},{5,4},{10,11},{11,10},{12,13},{13,12},{18,19},{1... | collective-permute-start | bytes 6291464 | tf_op jit(solution)/shard_map/ppermute | solution.py:107
  433.9 85.2 %collective-permute-start.20 = (bf16[4096,256]{1,0:T(8,128)(2,1)}, bf16[4096,256]{1,0:T(8,128)(2,1)}, u32[]{:S(2)}, u32[]{:S(2)}) collective-permute-start(bf16[4096,256]{1,0:T(8,128)(2,1)} %collective-permute-done.16), channel_id=1, source_target_pairs={{2,3},{3,2},{4,5},{5,4},{10,11},{11,10},{12,13},{13,12},{18,19},{1... | collective-permute-start | bytes 6291464 | tf_op jit(solution)/shard_map/ppermute | solution.py:107
  441.7 1.5 copy-start.2
  443.2 50.5 %copy-start.18 = (bf16[2048,512]{1,0:T(8,128)(2,1)S(1)}, bf16[2048,512]{1,0:T(8,128)(2,1)}, u32[]{:S(2)}) copy-start(bf16[2048,512]{1,0:T(8,128)(2,1)} %convolution_convert_fusion) | copy-start | bytes 6291460
  443.2 235.1 %reduce-scatter.11.cloned.1.call-start = ((), (), s32[]{:S(2)}) async-start(), calls=%async_computation.11 | async-start | bytes 2621440 | tf_op jit(solution)/shard_map/reduce_scatter | solution.py:112
  468.9 24.8 %copy-start.24 = (bf16[2048,512]{1,0:T(8,128)(2,1)S(1)}, bf16[2048,512]{1,0:T(8,128)(2,1)}, u32[]{:S(2)}) copy-start(bf16[2048,512]{1,0:T(8,128)(2,1)} %copy-done.21) | copy-start | bytes 6291460
  496.7 4.5 copy-start.25
  501.0 1.6 copy-start.19
  505.6 4.3 copy-start.20
  505.6 4.3 copy-start.26
  522.0 1.3 copy-start.3
  523.3 208.8 %reduce-scatter.5.cloned.1.call-start = ((), (), s32[]{:S(2)}) async-start(), calls=%async_computation.6 | async-start | bytes 2621440 | tf_op jit(solution)/shard_map/reduce_scatter | solution.py:112
  558.2 25.3 %copy-start.12 = (bf16[2048,512]{1,0:T(8,128)(2,1)S(1)}, bf16[2048,512]{1,0:T(8,128)(2,1)}, u32[]{:S(2)}) copy-start(bf16[2048,512]{1,0:T(8,128)(2,1)} %convolution_convert_fusion.3) | copy-start | bytes 6291460
  582.3 1.3 copy-start.27
  583.6 3.2 copy-start.11
  590.4 1.6 copy-start.13
  592.0 3.6 copy-start.28
  610.1 1.3 copy-start.4
  611.4 159.1 %reduce-scatter.7.cloned.1.call-start = ((), (), s32[]{:S(2)}) async-start(), calls=%async_computation.7 | async-start | bytes 2621440 | tf_op jit(solution)/shard_map/reduce_scatter | solution.py:112
  620.3 1.6 copy-start.14
  622.0 3.7 copy-start.29
  640.0 1.3 copy-start.1
  641.4 129.1 %collective-permute-start.21 = (bf16[2,256,512]{2,1,0:T(8,128)(2,1)}, bf16[2,256,512]{2,1,0:T(8,128)(2,1)S(1)}, u32[]{:S(2)}, u32[]{:S(2)}) collective-permute-start(bf16[2,256,512]{2,1,0:T(8,128)(2,1)} %reduce-scatter.9.cloned.1.call-done), channel_id=1, source_target_pairs={{2,0},{3,1},{4,6},{5,7},{10,8},{11,9},{12,14},{13,15},{18,16},{19,... | collective-permute-start | bytes 1572872 | tf_op jit(solution)/shard_map/ppermute | solution.py:114
  678.3 92.2 %collective-permute-start.22 = (bf16[2,256,512]{2,1,0:T(8,128)(2,1)}, bf16[2,256,512]{2,1,0:T(8,128)(2,1)S(1)}, u32[]{:S(2)}, u32[]{:S(2)}) collective-permute-start(bf16[2,256,512]{2,1,0:T(8,128)(2,1)} %reduce-scatter.11.cloned.1.call-done), channel_id=1, source_target_pairs={{2,0},{3,1},{4,6},{5,7},{10,8},{11,9},{12,14},{13,15},{18,16},{19,... | collective-permute-start | bytes 1572872 | tf_op jit(solution)/shard_map/ppermute | solution.py:114
  771.9 1.6 copy-start.8
Sparse Core Ops, SparseCore 0:
  201.1 88.7 all-gather.10
  291.7 87.6 all-gather.8
  381.2 87.6 all-gather.4
  470.6 87.6 all-gather.6
  561.1 62.9 reduce-scatter.8
  627.1 51.1 reduce-scatter.10
  681.3 50.7 reduce-scatter.4
  735.3 35.1 reduce-scatter.6

commit v2 on v1

v2 whole, which is shorter than its diff:
```python
import jax
import jax.numpy as jnp
from jax import lax
from jax.sharding import PartitionSpec as P

CORES = 2
HALVES = 2


def tie(value, other):
    if other is None:
        return value
    return lax.optimization_barrier((value, other))[0]


def dot(left, right):
    return lax.dot_general(left, right, (((0,), (0,)), ((), ())), preferred_element_type=jnp.float32).astype(jnp.bfloat16)


def make(n_aux, n_vir):
    line = n_vir // CORES
    shift = line // 4
    inner = 2 * shift
    outer_to_inner = [(g, g + shift) for g in range(shift)] + [(g, g - shift) for g in range(line - shift, line)]

    def on_cores(pairs):
        return [(a * CORES + c, b * CORES + c) for a, b in pairs for c in range(CORES)]

    hand = on_cores(outer_to_inner)
    back = [(b, a) for a, b in hand]
    swap = [(v, v ^ 1) for v in range(shift * CORES, (line - shift) * CORES)]

    def turn(r):
        return on_cores([(shift + j, shift + (j + r) % inner) for j in range(inner)])

    def shards(orbitals, screened, density_in):
        rows, occ, cols = orbitals.shape
        part = cols // HALVES
        v = lax.axis_index("vir")
        g, c = v // CORES, v % CORES
        is_inner = (g >= shift) & (g < line - shift)
        partner = jnp.where(g < line // 2, g - shift, g + shift)

        by_occ = jnp.transpose(orbitals, (1, 0, 2))
        halves = [by_occ[:, :, h * part : (h + 1) * part].reshape(occ * rows, part) for h in range(HALVES)]

        out_w = lax.ppermute(screened, "vir", hand)
        out_halves = []
        last = out_w
        for h in range(HALVES):
            last = lax.ppermute(tie(halves[h], last), "vir", hand)
            out_halves.append(last)

        def gather(block):
            return lax.all_gather(block, "aux", axis=0, tiled=True)

        own_rows = [gather(by_occ[0])]
        for i in range(1, occ):
            own_rows.append(gather(tie(by_occ[i], own_rows[-1])))
        out_rows = []
        for i in range(occ):
            block = jnp.concatenate([x[i * rows : (i + 1) * rows] for x in out_halves], axis=1)
            out_rows.append(gather(tie(block, out_rows[-1] if out_rows else own_rows[-1])))

        def source(r):
            own = shift + lax.rem(g - shift - r + 2 * inner, inner)
            return own, jnp.where(own < line // 2, own - shift, own + shift)

        flight = []

        def rotate(value, r, after):
            value = tie(value, flight[-1] if flight else None)
            flight.append(lax.ppermute(tie(value, after), "vir", turn(r)))
            return flight[-1]

        turns = range(1, inner)
        w_pieces = [(g, screened), (partner, out_w)]
        w_pieces += [(source(r)[0], rotate(screened, r, None)) for r in turns]
        w_pieces += [(source(r)[1], rotate(out_w, r, own_rows[0])) for r in turns]
        b_pieces = [[(g, halves[h]), (partner, out_halves[h])] for h in range(HALVES)]
        for h in range(HALVES):
            b_pieces[h] += [(source(r)[0], rotate(halves[h], r, own_rows[-1])) for r in turns]
        for h in range(HALVES):
            b_pieces[h] += [(source(r)[1], rotate(out_halves[h], r, out_rows[0])) for r in turns]

        depth = screened.shape[0]
        w_all = jnp.zeros((depth * n_vir, screened.shape[1]), screened.dtype)
        for place, piece in w_pieces:
            other = lax.ppermute(piece, "vir", swap)
            w_all = lax.dynamic_update_slice(w_all, piece, ((place * CORES + c) * depth, 0))
            w_all = lax.dynamic_update_slice(w_all, other, ((place * CORES + 1 - c) * depth, 0))

        right = [jnp.concatenate([dot(w_all, x) for x in side], axis=0) for side in (own_rows, out_rows)]

        left = []
        for h in range(HALVES):
            block = jnp.zeros((occ * rows, n_vir * part), orbitals.dtype)
            for place, piece in b_pieces[h]:
                other = lax.ppermute(piece, "vir", swap)
                block = lax.dynamic_update_slice(block, piece, (0, (place * CORES + c) * part))
                block = lax.dynamic_update_slice(block, other, (0, (place * CORES + 1 - c) * part))
            left.append(block)

        summed = [[], []]
        for side in (1, 0):
            for h in range(HALVES):
                mine = lax.psum_scatter(dot(left[h], right[side]), "aux", scatter_dimension=0, tiled=True)
                if side == 1:
                    mine = lax.ppermute(mine, "vir", back)
                summed[side].append(mine.reshape(-1, part, cols))
        total = [jnp.stack(x, axis=1).reshape(density_in.shape) for x in summed]
        return density_in + jnp.where(is_inner, total[0], total[1]).astype(jnp.float32)

    return shards


def solution(mesh):
    return jax.shard_map(
        make(mesh.shape["aux"], mesh.shape["vir"]),
        mesh=mesh,
        in_specs=(P("aux", None, "vir"), P("vir", "aux"), P("aux", "vir")),
        out_specs=P("aux", "vir"),
        check_vma=False,
    )
```

time: 790 us -> 911 us (1.15)
  waiting for transfers between devices: 423 us -> 574 us
  matrix products: 199 us -> 151 us
  local copies, waits for them, and re-layouts: 75.9 us -> 104 us
  starting transfers between devices: 60.6 us -> 51.4 us
    reduce_scatter x4, waiting for transfers between devices: 127 us -> 230 us  [shards(): lax.psum_scatter(dot(left[h], right[side]), 'aux', scatter_dimension=0, t...]
    dot_general x36 -> x8, matrix products: 199 us -> 151 us  [dot(): lax.dot_general(left, right, (((0,), (0,)), ((), ())), preferred_element_...]
    all_gather x4, waiting for transfers between devices: 129 us -> 170 us  [gather(): return lax.all_gather(block, 'aux', axis=0, tiled=True)]
    dynamic_update_slice x8 -> x16, local copies, waits for them, and re-layouts: 0.19 us -> 36.1 us  [the longest x8 22.8 us: shards(): lax.dynamic_update_slice(block, other, (0, (place * CORES + 1 - c) * part))]
    ppermute x14 -> x6, starting transfers between devices: 30 us -> 11.1 us  [rotate(): flight.append(lax.ppermute(tie(value, after), 'vir', turn(r)))]
    unnamed x61 -> x35, local copies, waits for them, and re-layouts: 20.3 us -> 6.59 us
    ppermute x4 -> x12, starting transfers between devices: 10.7 us -> 24.4 us  [shards(): other = lax.ppermute(piece, 'vir', swap)]
  transfers between devices with their start and end apart: 31 -> 31, of which waited for: 10 -> 9; matrix products, arithmetic and copies ran while one was open for 33% -> 28% of each run, Pallas kernels for 0% -> 0%
where the time goes in v2:
time: 911 us; the launch traced here: 903 us
  waiting for transfers between devices  574 us (63%)
  matrix products  151 us (17%)
  local copies, waits for them, and re-layouts  104 us (11%)
  starting transfers between devices  51.4 us (6%)
  between operations  14.3 us (2%)
    reduce_scatter x4, waiting for transfers between devices, shards(): lax.psum_scatter(dot(left[h], right[side]), 'aux', scatter_dimension=0, t...  230 us
    all_gather x4, waiting for transfers between devices, gather(): return lax.all_gather(block, 'aux', axis=0, tiled=True)  170 us
    dot_general x8, matrix products, dot(): lax.dot_general(left, right, (((0,), (0,)), ((), ())), preferred_element_...  151 us
    ppermute x1, waiting for transfers between devices, shards(): out_w = lax.ppermute(screened, 'vir', hand)  87.3 us
    ppermute x2, waiting for transfers between devices, shards(): last = lax.ppermute(tie(halves[h], last), 'vir', hand)  86.7 us
    ppermute x12, starting transfers between devices, shards(): other = lax.ppermute(piece, 'vir', swap)  24.4 us
    dynamic_update_slice x8, local copies, waits for them, and re-layouts, shards(): lax.dynamic_update_slice(block, other, (0, (place * CORES + 1 - c) * part))  22.8 us
    dynamic_update_slice x4, local copies, waits for them, and re-layouts, shards(): lax.dynamic_update_slice(w_all, other, ((place * CORES + 1 - c) * depth, 0))  19.6 us
  transfers between devices with their start and end apart: 31, of which 9 were waited for; matrix products, arithmetic and copies ran while one was open for 28% of the time, Pallas kernels for 0%

profile of v2, /device:TPU:0, one launch (start us, length us, event | category | flops | bytes accessed | tf_op | source)
XLA Modules:
  0.0 902.6 jit_solution(5339194694962479657)
XLA Ops:
  6.5 2.9 copy.8
  9.4 2.4 slice_bitcast_fusion
  12.8 90.4 %all-gather.12.cloned.1.call-done = bf16[1,8192,512]{2,1,0:T(8,128)(2,1)} async-done(((bf16[1,2048,512]{2,1,0:T(8,128)(2,1)}), bf16[1,8192,512]{2,1,0:T(8,128)(2,1)}) %all-gather.12.cloned.1.call-update) | async-done | bytes 8388624 | tf_op jit(solution)/shard_map/all_gather | solution.py:55
  103.3 3.7 collective-permute-start.1
  106.9 2.5 fusion.6
  109.4 87.3 %collective-permute-done.1 = bf16[1024,2048]{1,0:T(8,128)(2,1)S(1)} collective-permute-done((bf16[1024,2048]{1,0:T(8,128)(2,1)}, bf16[1024,2048]{1,0:T(8,128)(2,1)S(1)}, u32[]{:S(2)}, u32[]{:S(2)}) %collective-permute-start.1) | collective-permute-done | bytes 4194336 | tf_op jit(solution)/shard_map/ppermute | solution.py:47
  196.8 4.4 collective-permute-start.2
  201.2 43.9 %collective-permute-done.2 = bf16[4096,256]{1,0:T(8,128)(2,1)S(1)} collective-permute-done((bf16[4096,256]{1,0:T(8,128)(2,1)S(1)}, bf16[4096,256]{1,0:T(8,128)(2,1)S(1)}, u32[]{:S(2)}, u32[]{:S(2)}) %collective-permute-start.2) | collective-permute-done | bytes 2097184 | tf_op jit(solution)/shard_map/ppermute | solution.py:51
  245.1 4.5 collective-permute-start.9
  249.7 42.8 %collective-permute-done.9 = bf16[4096,256]{1,0:T(8,128)(2,1)S(1)} collective-permute-done((bf16[4096,256]{1,0:T(8,128)(2,1)S(1)}, bf16[4096,256]{1,0:T(8,128)(2,1)S(1)}, u32[]{:S(2)}, u32[]{:S(2)}) %collective-permute-start.9) | collective-permute-done | bytes 2097184 | tf_op jit(solution)/shard_map/ppermute | solution.py:51
  295.2 2.8 collective-permute-start.4
  298.0 2.7 collective-permute-start.5
  300.7 2.8 pad_maximum_fusion.7
  303.5 79.5 %all-gather.8.cloned.1.call-done = bf16[8192,512]{1,0:T(8,128)(2,1)} async-done(((bf16[2048,512]{1,0:T(8,128)(2,1)}), bf16[8192,512]{1,0:T(8,128)(2,1)}) %all-gather.8.cloned.1.call-update) | async-done | bytes 8388624 | tf_op jit(solution)/shard_map/all_gather | solution.py:55
  383.1 2.7 collective-permute-start.12
  385.8 2.0 collective-permute-start
  387.8 2.0 collective-permute-start.16
  389.8 2.6 collective-permute-start.13
  392.4 2.7 collective-permute-start.14
  395.1 7.4 broadcast.8.clone.1
  402.4 1.5 constant_dynamic-update-slice_fusion.23
  404.9 11.1 %broadcast_in_dim.3 = bf16[8192,2048]{1,0:T(8,128)(2,1)} broadcast(bf16[]{:T(256)} %constant.47.clone.1), dimensions={} | broadcast | bytes 33554432 | tf_op jit(solution)/shard_map/broadcast_in_dim | solution.py:87
  416.0 2.3 constant_dynamic-update-slice_fusion.15
  418.2 2.0 broadcast.8.clone
  420.7 2.7 collective-permute-start.15
  423.3 3.1 constant_dynamic-update-slice_fusion.22
  426.5 1.9 constant_dynamic-update-slice_fusion.6
  428.4 5.4 constant_dynamic-update-slice_fusion.14
  433.8 2.0 collective-permute-start.3
  435.8 2.0 collective-permute-start.8
  437.8 2.4 constant_dynamic-update-slice_fusion.13
  440.2 1.5 constant_dynamic-update-slice_fusion.21
  441.7 2.0 collective-permute-start.17
  443.7 4.7 constant_dynamic-update-slice_fusion.12
  448.5 4.8 constant_dynamic-update-slice_fusion.11
  453.3 4.7 constant_dynamic-update-slice_fusion.10
  460.0 5.4 constant_dynamic-update-slice_fusion.20
  465.4 5.6 constant_dynamic-update-slice_fusion.9
  470.9 4.8 constant_dynamic-update-slice_fusion.8
  475.7 1.6 constant_dynamic-update-slice_fusion.19
  477.3 2.0 collective-permute-start.18
  480.8 2.0 collective-permute-start.19
  483.8 24.7 %convolution_convert_fusion.1 = bf16[2048,512]{1,0:T(8,128)(2,1)} fusion(bf16[8192,2048]{1,0:T(8,128)(2,1)} %constant_dynamic-update-slice_fusion.8, bf16[8192,512]{1,0:T(8,128)(2,1)} %all-gather.8.cloned.1.call-done), kind=kOutput, calls=%fused_computation.4 | convolution fusion | flops 17180917760 | bytes 44040192 | tf_op jit(solution)/shard_map/dot_general | solution.py:17
  508.4 1.5 constant_dynamic-update-slice_fusion.17
  510.0 2.0 collective-permute-start.20
  512.0 1.5 constant_dynamic-update-slice_fusion.16
  513.5 24.0 %convolution_convert_fusion = bf16[2048,512]{1,0:T(8,128)(2,1)S(1)} fusion(bf16[8192,2048]{1,0:T(8,128)(2,1)} %constant_dynamic-update-slice_fusion.8, bf16[8192,512]{1,0:T(8,128)(2,1)} %all-gather.10.cloned.1.call-done), kind=kOutput, calls=%fused_computation.3 | convolution fusion | flops 17180917760 | bytes 44040192 | tf_op jit(solution)/shard_map/dot_general | solution.py:17
  538.8 13.5 %convolution_convert_fusion.5 = bf16[2048,512]{1,0:T(8,128)(2,1)} fusion(bf16[4096,2048]{1,0:T(8,128)(2,1)} %constant_dynamic-update-slice_fusion.16, bf16[2048,512]{1,0:T(8,128)(2,1)S(1)} %convolution_convert_fusion, bf16[2048,512]{1,0:T(8,128)(2,1)S(1)} %copy-done.12), kind=kOutput, calls=%fused_computation.8 | convolution fusion | flops 8599371776 | bytes 23068672 | tf_op jit(solution)/shard_map/dot_general | solution.py:17
  552.6 3.1 constant_dynamic-update-slice_fusion.4
  555.7 3.1 constant_dynamic-update-slice_fusion.3
  558.9 3.1 constant_dynamic-update-slice_fusion.2
  562.0 3.3 constant_dynamic-update-slice_fusion.1
  565.2 3.1 constant_dynamic-update-slice_fusion
  568.4 13.4 %convolution_convert_fusion.4 = bf16[2048,512]{1,0:T(8,128)(2,1)} fusion(bf16[4096,2048]{1,0:T(8,128)(2,1)} %constant_dynamic-update-slice_fusion, bf16[2048,512]{1,0:T(8,128)(2,1)S(1)} %copy-done.15, bf16[2048,512]{1,0:T(8,128)(2,1)S(1)} %copy-done.13), kind=kOutput, calls=%fused_computation.7 | convolution fusion | flops 8599371776 | bytes 23068672 | tf_op jit(solution)/shard_map/dot_general | solution.py:17
  581.9 23.9 %convolution_convert_fusion.3 = bf16[2048,512]{1,0:T(8,128)(2,1)S(1)} fusion(bf16[8192,2048]{1,0:T(8,128)(2,1)} %constant_dynamic-update-slice_fusion.8, bf16[1,8192,512]{2,1,0:T(8,128)(2,1)} %all-gather.12.cloned.1.call-done), kind=kOutput, calls=%fused_computation.6 | convolution fusion | flops 17180917760 | bytes 44040192 | tf_op jit(solution)/shard_map/dot_general | solution.py:17
  605.8 23.9 %convolution_convert_fusion.2 = bf16[2048,512]{1,0:T(8,128)(2,1)S(1)} fusion(bf16[8192,2048]{1,0:T(8,128)(2,1)} %constant_dynamic-update-slice_fusion.8, bf16[8192,512]{1,0:T(8,128)(2,1)} %all-gather.6.cloned.1.call-done), kind=kOutput, calls=%fused_computation.5 | convolution fusion | flops 17180917760 | bytes 44040192 | tf_op jit(solution)/shard_map/dot_general | solution.py:17
  631.0 13.4 %convolution_convert_fusion.7 = bf16[2048,512]{1,0:T(8,128)(2,1)} fusion(bf16[4096,2048]{1,0:T(8,128)(2,1)} %constant_dynamic-update-slice_fusion.16, bf16[2048,512]{1,0:T(8,128)(2,1)S(1)} %convolution_convert_fusion.2, bf16[2048,512]{1,0:T(8,128)(2,1)S(1)} %convolution_convert_fusion.3), kind=kOutput, calls=%fused_computation.10 | convolution fusion | flops 8599371776 | bytes 23068672 | tf_op jit(solution)/shard_map/dot_general | solution.py:17
  644.7 14.1 %convolution_convert_fusion.6 = bf16[2048,512]{1,0:T(8,128)(2,1)} fusion(bf16[4096,2048]{1,0:T(8,128)(2,1)} %constant_dynamic-update-slice_fusion, bf16[2048,512]{1,0:T(8,128)(2,1)} %copy-done.16, bf16[2048,512]{1,0:T(8,128)(2,1)S(1)} %convolution_convert_fusion.3), kind=kOutput, calls=%fused_computation.9 | convolution fusion | flops 8599371776 | bytes 23068672 | tf_op jit(solution)/shard_map/dot_general | solution.py:17
  658.8 101.5 %reduce-scatter.9.cloned.1.call-done = bf16[512,512]{1,0:T(8,128)(2,1)} async-done(((bf16[2048,512]{1,0:T(8,128)(2,1)}), bf16[512,512]{1,0:T(8,128)(2,1)}) %reduce-scatter.9.cloned.1.call-update) | async-done | bytes 524304 | tf_op jit(solution)/shard_map/reduce_scatter | solution.py:107
  761.6 37.0 %reduce-scatter.11.cloned.1.call-done = bf16[512,512]{1,0:T(8,128)(2,1)} async-done(((bf16[2048,512]{1,0:T(8,128)(2,1)}), bf16[512,512]{1,0:T(8,128)(2,1)}) %reduce-scatter.11.cloned.1.call-update) | async-done | bytes 524304 | tf_op jit(solution)/shard_map/reduce_scatter | solution.py:107
  800.0 53.2 %reduce-scatter.5.cloned.1.call-done = bf16[512,512]{1,0:T(8,128)(2,1)} async-done(((bf16[2048,512]{1,0:T(8,128)(2,1)}), bf16[512,512]{1,0:T(8,128)(2,1)}) %reduce-scatter.5.cloned.1.call-update) | async-done | bytes 524304 | tf_op jit(solution)/shard_map/reduce_scatter | solution.py:107
  853.2 38.5 %reduce-scatter.7.cloned.1.call-done = bf16[512,512]{1,0:T(8,128)(2,1)} async-done(((bf16[2048,512]{1,0:T(8,128)(2,1)}), bf16[512,512]{1,0:T(8,128)(2,1)}) %reduce-scatter.7.cloned.1.call-update) | async-done | bytes 524304 | tf_op jit(solution)/shard_map/reduce_scatter | solution.py:107
  891.7 1.5 fusion
  893.6 1.8 bitcast_add_fusion
  (85 shorter events, 15.8 us)
Async XLA Ops:
  6.5 96.7 %all-gather.12.cloned.1.call-start = ((), (), s32[]{:S(2)}) async-start(), calls=%async_computation.11 | async-start | bytes 10485760 | tf_op jit(solution)/shard_map/all_gather | solution.py:55
  9.4 3.3 copy-start
  12.7 282.4 %all-gather.6.cloned.1.call-start = ((), (), s32[]{:S(2)}) async-start(), calls=%async_computation.4 | async-start | bytes 10485760 | tf_op jit(solution)/shard_map/all_gather | solution.py:55
  103.2 279.8 %all-gather.8.cloned.1.call-start = ((), (), s32[]{:S(2)}) async-start(), calls=%async_computation.5 | async-start | bytes 10485760 | tf_op jit(solution)/shard_map/all_gather | solution.py:55
  103.3 93.5 %collective-permute-start.1 = (bf16[1024,2048]{1,0:T(8,128)(2,1)}, bf16[1024,2048]{1,0:T(8,128)(2,1)S(1)}, u32[]{:S(2)}, u32[]{:S(2)}) collective-permute-start(bf16[1024,2048]{1,0:T(8,128)(2,1)} %param.4), channel_id=1, source_target_pairs={{0,2},{1,3},{6,4},{7,5},{8,10},{9,11},{14,12},{15,13},{16,18},{17,... | collective-permute-start | bytes 12582920 | tf_op jit(solution)/shard_map/ppermute | solution.py:47
  109.4 135.6 %copy-start.6 = (bf16[2,2048,256]{2,1,0:T(8,128)(2,1)}, bf16[2,2048,256]{2,1,0:T(8,128)(2,1)S(1)}, u32[]{:S(2)}) copy-start(bf16[2,2048,256]{2,1,0:T(8,128)(2,1)S(1)} %get-tuple-element.37) | copy-start | bytes 6291460
  109.4 184.2 %copy-start.4 = (bf16[2,2048,256]{2,1,0:T(8,128)(2,1)}, bf16[2,2048,256]{2,1,0:T(8,128)(2,1)S(1)}, u32[]{:S(2)}) copy-start(bf16[2,2048,256]{2,1,0:T(8,128)(2,1)S(1)} %get-tuple-element.38) | copy-start | bytes 6291460
  196.8 96.9 %copy-start.9 = (bf16[1024,2048]{1,0:T(8,128)(2,1)}, bf16[1024,2048]{1,0:T(8,128)(2,1)S(1)}, u32[]{:S(2)}) copy-start(bf16[1024,2048]{1,0:T(8,128)(2,1)S(1)} %collective-permute-done.1) | copy-start | bytes 12582916
  196.8 48.3 %collective-permute-start.2 = (bf16[4096,256]{1,0:T(8,128)(2,1)S(1)}, bf16[4096,256]{1,0:T(8,128)(2,1)S(1)}, u32[]{:S(2)}, u32[]{:S(2)}) collective-permute-start(bf16[4096,256]{1,0:T(8,128)(2,1)S(1)} %bitcast.33), channel_id=1, source_target_pairs={{0,2},{1,3},{6,4},{7,5},{8,10},{9,11},{14,12},{15,13},{16,18},{17,... | collective-permute-start | bytes 6291464 | tf_op jit(solution)/shard_map/ppermute | solution.py:51
  245.1 48.6 %copy-start.2 = (bf16[4096,256]{1,0:T(8,128)(2,1)}, bf16[4096,256]{1,0:T(8,128)(2,1)S(1)}, u32[]{:S(2)}) copy-start(bf16[4096,256]{1,0:T(8,128)(2,1)S(1)} %collective-permute-done.2) | copy-start | bytes 6291460
  245.1 47.5 %collective-permute-start.9 = (bf16[4096,256]{1,0:T(8,128)(2,1)S(1)}, bf16[4096,256]{1,0:T(8,128)(2,1)S(1)}, u32[]{:S(2)}, u32[]{:S(2)}) collective-permute-start(bf16[4096,256]{1,0:T(8,128)(2,1)S(1)} %bitcast.29), channel_id=1, source_target_pairs={{0,2},{1,3},{6,4},{7,5},{8,10},{9,11},{14,12},{15,13},{16,18},{17,... | collective-permute-start | bytes 6291464 | tf_op jit(solution)/shard_map/ppermute | solution.py:51
  295.2 218.3 %all-gather.10.cloned.1.call-start = ((), (), s32[]{:S(2)}) async-start(), calls=%async_computation.8 | async-start | bytes 10485760 | tf_op jit(solution)/shard_map/all_gather | solution.py:55
  295.2 2.8 collective-permute-start.4
  298.0 94.4 %collective-permute-start.5 = (bf16[1024,2048]{1,0:T(8,128)(2,1)}, bf16[1024,2048]{1,0:T(8,128)(2,1)}, u32[]{:S(2)}, u32[]{:S(2)}) collective-permute-start(bf16[1024,2048]{1,0:T(8,128)(2,1)} %copy-done.9), channel_id=1, source_target_pairs={{2,4},{3,5},{4,2},{5,3},{10,12},{11,13},{12,10},{13,11},{18,20},{1... | collective-permute-start | bytes 12582920 | tf_op jit(solution)/shard_map/ppermute | solution.py:73
  383.1 377.3 %reduce-scatter.9.cloned.1.call-start = ((), (), s32[]{:S(2)}) async-start(), calls=%async_computation.9 | async-start | bytes 2621440 | tf_op jit(solution)/shard_map/reduce_scatter | solution.py:107
  383.1 45.3 %collective-permute-start.12 = (bf16[1024,2048]{1,0:T(8,128)(2,1)}, bf16[1024,2048]{1,0:T(8,128)(2,1)}, u32[]{:S(2)}, u32[]{:S(2)}) collective-permute-start(bf16[1024,2048]{1,0:T(8,128)(2,1)} %param.4), channel_id=1, source_target_pairs={{2,3},{3,2},{4,5},{5,4},{10,11},{11,10},{12,13},{13,12},{18,19},{1... | collective-permute-start | bytes 12582920 | tf_op jit(solution)/shard_map/ppermute | solution.py:89
  385.8 18.2 %collective-permute-start = (bf16[4096,256]{1,0:T(8,128)(2,1)}, bf16[4096,256]{1,0:T(8,128)(2,1)}, u32[]{:S(2)}, u32[]{:S(2)}) collective-permute-start(bf16[4096,256]{1,0:T(8,128)(2,1)} %bitcast.34), channel_id=1, source_target_pairs={{2,3},{3,2},{4,5},{5,4},{10,11},{11,10},{12,13},{13,12},{18,19},{1... | collective-permute-start | bytes 6291464 | tf_op jit(solution)/shard_map/ppermute | solution.py:99
  387.8 32.9 %collective-permute-start.16 = (bf16[4096,256]{1,0:T(8,128)(2,1)}, bf16[4096,256]{1,0:T(8,128)(2,1)}, u32[]{:S(2)}, u32[]{:S(2)}) collective-permute-start(bf16[4096,256]{1,0:T(8,128)(2,1)} %bitcast.30), channel_id=1, source_target_pairs={{2,3},{3,2},{4,5},{5,4},{10,11},{11,10},{12,13},{13,12},{18,19},{1... | collective-permute-start | bytes 6291464 | tf_op jit(solution)/shard_map/ppermute | solution.py:99
  389.8 51.9 %collective-permute-start.13 = (bf16[1024,2048]{1,0:T(8,128)(2,1)}, bf16[1024,2048]{1,0:T(8,128)(2,1)}, u32[]{:S(2)}, u32[]{:S(2)}) collective-permute-start(bf16[1024,2048]{1,0:T(8,128)(2,1)} %copy-done.9), channel_id=1, source_target_pairs={{2,3},{3,2},{4,5},{5,4},{10,11},{11,10},{12,13},{13,12},{18,19},{1... | collective-permute-start | bytes 12582920 | tf_op jit(solution)/shard_map/ppermute | solution.py:89
  392.4 60.9 %collective-permute-start.14 = (bf16[1024,2048]{1,0:T(8,128)(2,1)}, bf16[1024,2048]{1,0:T(8,128)(2,1)}, u32[]{:S(2)}, u32[]{:S(2)}) collective-permute-start(bf16[1024,2048]{1,0:T(8,128)(2,1)} %collective-permute-done.4), channel_id=1, source_target_pairs={{2,3},{3,2},{4,5},{5,4},{10,11},{11,10},{12,13},{13,12},{18,19},{1... | collective-permute-start | bytes 12582920 | tf_op jit(solution)/shard_map/ppermute | solution.py:89
  395.1 7.4 copy-start.7
  404.0 12.0 %copy-start.8 = (bf16[1024,2048]{1,0:T(8,128)(2,1)S(1)}, bf16[1024,2048]{1,0:T(8,128)(2,1)}, u32[]{:S(2)}) copy-start(bf16[1024,2048]{1,0:T(8,128)(2,1)} %param.4) | copy-start | bytes 12582916
  404.0 31.8 %collective-permute-start.6 = (bf16[4096,256]{1,0:T(8,128)(2,1)S(1)}, bf16[4096,256]{1,0:T(8,128)(2,1)S(1)}, u32[]{:S(2)}, u32[]{:S(2)}) collective-permute-start(bf16[4096,256]{1,0:T(8,128)(2,1)S(1)} %bitcast.36), channel_id=1, source_target_pairs={{2,4},{3,5},{4,2},{5,3},{10,12},{11,13},{12,10},{13,11},{18,20},{1... | collective-permute-start | bytes 6291464 | tf_op jit(solution)/shard_map/ppermute | solution.py:73
  418.2 2.1 copy-start.5
  420.7 50.3 %collective-permute-start.15 = (bf16[1024,2048]{1,0:T(8,128)(2,1)}, bf16[1024,2048]{1,0:T(8,128)(2,1)}, u32[]{:S(2)}, u32[]{:S(2)}) collective-permute-start(bf16[1024,2048]{1,0:T(8,128)(2,1)} %collective-permute-done.5), channel_id=1, source_target_pairs={{2,3},{3,2},{4,5},{5,4},{10,11},{11,10},{12,13},{13,12},{18,19},{1... | collective-permute-start | bytes 12582920 | tf_op jit(solution)/shard_map/ppermute | solution.py:89
  428.4 5.4 copy-start.3
  428.4 9.4 %copy-start.10 = (bf16[1024,2048]{1,0:T(8,128)(2,1)S(1)}, bf16[1024,2048]{1,0:T(8,128)(2,1)}, u32[]{:S(2)}) copy-start(bf16[1024,2048]{1,0:T(8,128)(2,1)} %copy-done.9) | copy-start | bytes 12582916
  433.8 26.2 %collective-permute-start.3 = (bf16[4096,256]{1,0:T(8,128)(2,1)S(1)}, bf16[4096,256]{1,0:T(8,128)(2,1)}, u32[]{:S(2)}, u32[]{:S(2)}) collective-permute-start(bf16[4096,256]{1,0:T(8,128)(2,1)S(1)} %copy-done.3), channel_id=1, source_target_pairs={{2,3},{3,2},{4,5},{5,4},{10,11},{11,10},{12,13},{13,12},{18,19},{1... | collective-permute-start | bytes 6291464 | tf_op jit(solution)/shard_map/ppermute | solution.py:99
  435.8 23.4 %collective-permute-start.8 = (bf16[4096,256]{1,0:T(8,128)(2,1)S(1)}, bf16[4096,256]{1,0:T(8,128)(2,1)}, u32[]{:S(2)}, u32[]{:S(2)}) collective-permute-start(bf16[4096,256]{1,0:T(8,128)(2,1)S(1)} %bitcast.32), channel_id=1, source_target_pairs={{2,4},{3,5},{4,2},{5,3},{10,12},{11,13},{12,10},{13,11},{18,20},{1... | collective-permute-start | bytes 6291464 | tf_op jit(solution)/shard_map/ppermute | solution.py:73
  441.7 110.9 %collective-permute-start.17 = (bf16[4096,256]{1,0:T(8,128)(2,1)S(1)}, bf16[4096,256]{1,0:T(8,128)(2,1)}, u32[]{:S(2)}, u32[]{:S(2)}) collective-permute-start(bf16[4096,256]{1,0:T(8,128)(2,1)S(1)} %collective-permute-done.9), channel_id=1, source_target_pairs={{2,3},{3,2},{4,5},{5,4},{10,11},{11,10},{12,13},{13,12},{18,19},{1... | collective-permute-start | bytes 6291464 | tf_op jit(solution)/shard_map/ppermute | solution.py:99
  458.0 21.3 %collective-permute-start.7 = (bf16[4096,256]{1,0:T(8,128)(2,1)S(1)}, bf16[4096,256]{1,0:T(8,128)(2,1)S(1)}, u32[]{:S(2)}, u32[]{:S(2)}) collective-permute-start(bf16[4096,256]{1,0:T(8,128)(2,1)S(1)} %collective-permute-done.6), channel_id=1, source_target_pairs={{2,3},{3,2},{4,5},{5,4},{10,11},{11,10},{12,13},{13,12},{18,19},{1... | collective-permute-start | bytes 6291464 | tf_op jit(solution)/shard_map/ppermute | solution.py:99
  459.2 18.2 %copy-start.1 = (bf16[4096,2048]{1,0:T(8,128)(2,1)}, bf16[4096,2048]{1,0:T(8,128)(2,1)S(1)}, u32[]{:S(2)}) copy-start(bf16[4096,2048]{1,0:T(8,128)(2,1)S(1)} %constant_dynamic-update-slice_fusion.5) | copy-start | bytes 50331652
  459.2 21.6 %collective-permute-start.10 = (bf16[4096,256]{1,0:T(8,128)(2,1)S(1)}, bf16[4096,256]{1,0:T(8,128)(2,1)S(1)}, u32[]{:S(2)}, u32[]{:S(2)}) collective-permute-start(bf16[4096,256]{1,0:T(8,128)(2,1)S(1)} %copy-done.3), channel_id=1, source_target_pairs={{2,4},{3,5},{4,2},{5,3},{10,12},{11,13},{12,10},{13,11},{18,20},{1... | collective-permute-start | bytes 6291464 | tf_op jit(solution)/shard_map/ppermute | solution.py:73
  477.3 81.5 %collective-permute-start.18 = (bf16[4096,256]{1,0:T(8,128)(2,1)}, bf16[4096,256]{1,0:T(8,128)(2,1)}, u32[]{:S(2)}, u32[]{:S(2)}) collective-permute-start(bf16[4096,256]{1,0:T(8,128)(2,1)} %collective-permute-done.8), channel_id=1, source_target_pairs={{2,3},{3,2},{4,5},{5,4},{10,11},{11,10},{12,13},{13,12},{18,19},{1... | collective-permute-start | bytes 6291464 | tf_op jit(solution)/shard_map/ppermute | solution.py:99
  480.8 29.2 %collective-permute-start.19 = (bf16[4096,256]{1,0:T(8,128)(2,1)S(1)}, bf16[4096,256]{1,0:T(8,128)(2,1)}, u32[]{:S(2)}, u32[]{:S(2)}) collective-permute-start(bf16[4096,256]{1,0:T(8,128)(2,1)S(1)} %collective-permute-done.9), channel_id=1, source_target_pairs={{2,4},{3,5},{4,2},{5,3},{10,12},{11,13},{12,10},{13,11},{18,20},{1... | collective-permute-start | bytes 6291464 | tf_op jit(solution)/shard_map/ppermute | solution.py:73
  482.8 29.2 %collective-permute-start.11 = (bf16[4096,256]{1,0:T(8,128)(2,1)S(1)}, bf16[4096,256]{1,0:T(8,128)(2,1)S(1)}, u32[]{:S(2)}, u32[]{:S(2)}) collective-permute-start(bf16[4096,256]{1,0:T(8,128)(2,1)S(1)} %collective-permute-done.10), channel_id=1, source_target_pairs={{2,3},{3,2},{4,5},{5,4},{10,11},{11,10},{12,13},{13,12},{18,19},{1... | collective-permute-start | bytes 6291464 | tf_op jit(solution)/shard_map/ppermute | solution.py:99
  510.0 55.3 %collective-permute-start.20 = (bf16[4096,256]{1,0:T(8,128)(2,1)}, bf16[4096,256]{1,0:T(8,128)(2,1)}, u32[]{:S(2)}, u32[]{:S(2)}) collective-permute-start(bf16[4096,256]{1,0:T(8,128)(2,1)} %collective-permute-done.19), channel_id=1, source_target_pairs={{2,3},{3,2},{4,5},{5,4},{10,11},{11,10},{12,13},{13,12},{18,19},{1... | collective-permute-start | bytes 6291464 | tf_op jit(solution)/shard_map/ppermute | solution.py:99
  513.5 25.3 %copy-start.12 = (bf16[2048,512]{1,0:T(8,128)(2,1)S(1)}, bf16[2048,512]{1,0:T(8,128)(2,1)}, u32[]{:S(2)}) copy-start(bf16[2048,512]{1,0:T(8,128)(2,1)} %convolution_convert_fusion.1) | copy-start | bytes 6291460
  537.5 1.3 copy-start.14
  552.4 246.3 %reduce-scatter.11.cloned.1.call-start = ((), (), s32[]{:S(2)}) async-start(), calls=%async_computation.10 | async-start | bytes 2621440 | tf_op jit(solution)/shard_map/reduce_scatter | solution.py:107
  562.0 6.4 copy-start.13
  562.0 6.4 copy-start.15
  581.9 271.3 %reduce-scatter.5.cloned.1.call-start = ((), (), s32[]{:S(2)}) async-start(), calls=%async_computation.6 | async-start | bytes 2621440 | tf_op jit(solution)/shard_map/reduce_scatter | solution.py:107
  629.7 1.3 copy-start.16
  644.4 247.2 %reduce-scatter.7.cloned.1.call-start = ((), (), s32[]{:S(2)}) async-start(), calls=%async_computation.7 | async-start | bytes 2621440 | tf_op jit(solution)/shard_map/reduce_scatter | solution.py:107
  760.3 131.3 %collective-permute-start.21 = (bf16[512,512]{1,0:T(8,128)(2,1)}, bf16[512,512]{1,0:T(8,128)(2,1)S(1)}, u32[]{:S(2)}, u32[]{:S(2)}) collective-permute-start(bf16[512,512]{1,0:T(8,128)(2,1)} %reduce-scatter.9.cloned.1.call-done), channel_id=1, source_target_pairs={{2,0},{3,1},{4,6},{5,7},{10,8},{11,9},{12,14},{13,15},{18,16},{19,... | collective-permute-start | bytes 1572872 | tf_op jit(solution)/shard_map/ppermute | solution.py:109
  798.7 93.0 %collective-permute-start.22 = (bf16[512,512]{1,0:T(8,128)(2,1)}, bf16[512,512]{1,0:T(8,128)(2,1)S(1)}, u32[]{:S(2)}, u32[]{:S(2)}) collective-permute-start(bf16[512,512]{1,0:T(8,128)(2,1)} %reduce-scatter.11.cloned.1.call-done), channel_id=1, source_target_pairs={{2,0},{3,1},{4,6},{5,7},{10,8},{11,9},{12,14},{13,15},{18,16},{19,... | collective-permute-start | bytes 1572872 | tf_op jit(solution)/shard_map/ppermute | solution.py:109
  891.7 1.9 copy-start.11
Sparse Core Ops, SparseCore 0:
  12.8 90.2 all-gather.11
  105.0 87.5 all-gather.5
  295.3 87.6 all-gather.7
  384.7 95.3 all-gather.9
  552.5 207.8 reduce-scatter.8
  763.4 35.1 reduce-scatter.10
  801.6 51.4 reduce-scatter.4
  856.4 35.2 reduce-scatter.6
